TPU v7x, 256 devices: a whole 4x4x8 slice. The times are simulated.
256 devices in a mesh: row: 32 (over y, x, core), col: 8 (over z).
Axes of the slice: x: 4, y: 4, z: 8, core: 2. Of those that a mesh axis runs over, the one named last changes fastest.
Arguments:
- tokens: bfloat16 [512, 12288], P('row', 'col'), may hold values from -6 to 6
- weight_in: bfloat16 [12288, 24576], P('col', 'row'), may hold values from -0.0546875 to 0.0546875
- weight_out: bfloat16 [24576, 12288], P('row', 'col'), may hold values from -0.0390625 to 0.0390625
- cotangent: bfloat16 [512, 12288], P('row', 'col'), may hold values from -1.5 to 1.5
Outputs:
- output: bfloat16 [512, 12288], P('row', 'col')
- grad_tokens: bfloat16 [512, 12288], P('row', 'col')
- grad_weight_in: bfloat16 [12288, 24576], P('col', 'row')
- grad_weight_out: bfloat16 [24576, 12288], P('row', 'col')
All inputs are finite; a program needn't handle non-finite values.
Results may differ from a plain program's by a relative error of at most 0.005.
Values may be sent and summed in bfloat16 or wider, within the bound.
A program may use at most 64 MiB of HBM per device.

v0:
```python
import jax
import jax.numpy as jnp
from jax import lax
from jax.sharding import PartitionSpec as P

gelu_scale = 0.7978845608028654
gelu_cubic = 0.044715


def activate(hidden):
    tangent = jnp.tanh(gelu_scale * (hidden + gelu_cubic * hidden * hidden * hidden))
    gelu_out = 0.5 * hidden * (1.0 + tangent)
    derivative = 0.5 * (1.0 + tangent) + 0.5 * hidden * (1.0 - tangent * tangent) * gelu_scale * (
        1.0 + 3.0 * gelu_cubic * hidden * hidden
    )
    return (gelu_out, derivative)


def contract_rows(left, right):
    return lax.dot_general(
        left, right, (((0,), (0,)), ((), ())), preferred_element_type=jnp.float32
    )


def contract_cols(left, right):
    return lax.dot_general(
        left, right, (((1,), (1,)), ((), ())), preferred_element_type=jnp.float32
    )


def per_device(tokens, weight_in, weight_out, cotangent):
    tok_all = lax.all_gather(tokens, "row", axis=0, tiled=True)
    panel = tok_all
    hidden = lax.psum_scatter(
        jnp.dot(panel, weight_in, preferred_element_type=jnp.float32),
        "col",
        scatter_dimension=0,
        tiled=True,
    )
    gelu_out, derivative = activate(hidden)
    act_all = lax.all_gather(gelu_out.astype(jnp.bfloat16), "col", axis=0, tiled=True)
    panel = act_all
    output = lax.psum_scatter(
        jnp.dot(panel, weight_out, preferred_element_type=jnp.float32),
        "row",
        scatter_dimension=0,
        tiled=True,
    ).astype(jnp.bfloat16)
    cot_all = lax.all_gather(cotangent, "row", axis=0, tiled=True)
    panel = cot_all
    grad_act = lax.psum_scatter(
        contract_cols(panel, weight_out), "col", scatter_dimension=0, tiled=True
    )
    grad_hidden = (grad_act * derivative).astype(jnp.bfloat16)
    grad_all = lax.all_gather(grad_hidden, "col", axis=0, tiled=True)
    grad_weight_out = contract_rows(act_all, cot_all).astype(jnp.bfloat16)
    panel = grad_all
    grad_tokens = lax.psum_scatter(
        contract_cols(panel, weight_in), "row", scatter_dimension=0, tiled=True
    ).astype(jnp.bfloat16)
    grad_weight_in = contract_rows(tok_all, grad_all).astype(jnp.bfloat16)
    return (output, grad_tokens, grad_weight_in, grad_weight_out)


def solution(mesh):
    in_specs = (P("row", "col"), P("col", "row"), P("row", "col"), P("row", "col"))
    out_specs = (P("row", "col"), P("row", "col"), P("col", "row"), P("row", "col"))
    return jax.shard_map(
        per_device, mesh=mesh, in_specs=in_specs, out_specs=out_specs, check_vma=False
    )
```

profile of v0, /device:TPU:2, one launch (start us, length us, event | category | flops | bytes accessed | tf_op | source)
XLA Modules:
  0.0 414.2 jit_solution(13101811578193887887)
XLA Ops:
  7.2 0.0 copy-start
  7.2 0.0 all-gather.5.cloned.1.call-start
  7.2 0.7 all-gather.5.cloned.1.call-update
  7.9 0.0 all-gather.3.cloned.1.call-start
  8.0 0.7 all-gather.3.cloned.1.call-update
  8.7 0.0 reduce-scatter.9.cloned.1.call-start
  8.7 52.8 %all-gather.5.cloned.1.call-done = bf16[512,1536]{1,0:T(8,128)(2,1)} async-done(((bf16[16,1536]{1,0:T(8,128)(2,1)}), bf16[512,1536]{1,0:T(8,128)(2,1)}) %all-gather.5.cloned.1.call-update) | async-done | bytes 1572880 | tf_op jit(solution)/shard_map/all_gather | solution.py:49
  61.5 0.0 copy-done
  61.5 4.0 fusion.10
  65.4 0.0 reduce-scatter.9.cloned.1.call-update
  65.5 0.0 reduce-scatter.5.cloned.1.call-start
  65.5 46.2 %all-gather.3.cloned.1.call-done = bf16[512,1536]{1,0:T(8,128)(2,1)} async-done(((bf16[16,1536]{1,0:T(8,128)(2,1)}), bf16[512,1536]{1,0:T(8,128)(2,1)}) %all-gather.3.cloned.1.call-update) | async-done | bytes 1572880 | tf_op jit(solution)/shard_map/all_gather | solution.py:32
  111.7 4.7 %fusion.8 = f32[512,768]{1,0:T(8,128)} fusion(bf16[512,1536]{1,0:T(8,128)(2,1)} %all-gather.3.cloned.1.call-done, bf16[1536,768]{1,0:T(8,128)(2,1)} %param.5), kind=kOutput, calls=%fused_computation.13 | convolution fusion | flops 1207959552 | bytes 5505024 | tf_op jit(solution)/shard_map/dot_general | solution.py:35
  116.4 0.0 reduce-scatter.5.cloned.1.call-update
  116.4 0.0 reduce-scatter.7.cloned.1.call-start
  116.4 38.6 %reduce-scatter.9.cloned.1.call-done = f32[64,768]{1,0:T(8,128)} async-done(((f32[512,768]{1,0:T(8,128)}), f32[64,768]{1,0:T(8,128)}) %reduce-scatter.9.cloned.1.call-update) | async-done | bytes 196624 | tf_op jit(solution)/shard_map/reduce_scatter | solution.py:51
  155.0 42.0 %reduce-scatter.5.cloned.1.call-done = f32[64,768]{1,0:T(8,128)} async-done(((f32[512,768]{1,0:T(8,128)}), f32[64,768]{1,0:T(8,128)}) %reduce-scatter.5.cloned.1.call-update) | async-done | bytes 196624 | tf_op jit(solution)/shard_map/reduce_scatter | solution.py:34
  197.1 1.2 fusion.7
  198.2 26.1 %all_gather.13 = bf16[512,768]{1,0:T(8,128)(2,1)S(1)} all-gather(bf16[64,768]{1,0:T(8,128)(2,1)S(1)} %get-tuple-element.9), channel_id=1, replica_groups=mesh['row'=32,'col'=8] {'col'}, dimensions={0}, use_global_device_ids=true | all-gather | bytes 884736 | tf_op jit(solution)/shard_map/all_gather | solution.py:41
  224.4 3.0 fusion.9
  227.4 0.0 reduce-scatter.7.cloned.1.call-update
  227.4 0.0 reduce-scatter.11.cloned.1.call-start
  227.5 25.8 %all_gather.15 = bf16[512,768]{1,0:T(8,128)(2,1)S(1)} all-gather(bf16[64,768]{1,0:T(8,128)(2,1)S(1)} %get-tuple-element.8), channel_id=1, replica_groups=mesh['row'=32,'col'=8] {'col'}, dimensions={0}, use_global_device_ids=true | all-gather | bytes 884736 | tf_op jit(solution)/shard_map/all_gather | solution.py:55
  253.2 0.0 copy-start.1
  253.2 0.9 copy-done.1
  254.1 4.8 %fusion.11 = f32[512,1536]{1,0:T(8,128)} fusion(bf16[512,768]{1,0:T(8,128)(2,1)S(1)} %all_gather.15, bf16[1536,768]{1,0:T(8,128)(2,1)} %param.5), kind=kOutput, calls=%fused_computation.16 | convolution fusion | flops 1207959552 | bytes 6291456 | tf_op jit(solution)/shard_map/dot_general | solution.py:26
  258.9 0.0 reduce-scatter.11.cloned.1.call-update
  259.0 4.5 %fusion = bf16[1536,768]{0,1:T(8,128)(2,1)} fusion(bf16[512,768]{1,0:T(8,128)(2,1)} %copy-done.1, bf16[512,1536]{1,0:T(8,128)(2,1)} %all-gather.3.cloned.1.call-done), kind=kOutput, calls=%fused_computation.2 | convolution fusion | flops 1209139200 | bytes 4718592 | tf_op jit(solution)/shard_map/dot_general | solution.py:20
  263.5 4.3 %copy.8 = bf16[1536,768]{1,0:T(8,128)(2,1)} copy(bf16[1536,768]{0,1:T(8,128)(2,1)} %fusion) | data formatting | bytes 4718592
  267.8 4.2 %convolution_convert_fusion = bf16[768,1536]{1,0:T(8,128)(2,1)} fusion(bf16[512,768]{1,0:T(8,128)(2,1)S(1)} %all_gather.13, bf16[512,1536]{1,0:T(8,128)(2,1)} %all-gather.5.cloned.1.call-done), kind=kOutput, calls=%fused_computation | convolution fusion | flops 1209139200 | bytes 4718592 | tf_op jit(solution)/shard_map/dot_general | solution.py:20
  272.0 42.1 %reduce-scatter.7.cloned.1.call-done = f32[16,1536]{1,0:T(8,128)} async-done(((f32[512,1536]{1,0:T(8,128)}), f32[16,1536]{1,0:T(8,128)}) %reduce-scatter.7.cloned.1.call-update) | async-done | bytes 98320 | tf_op jit(solution)/shard_map/reduce_scatter | solution.py:43
  314.1 1.5 convert_element_type.22
  315.6 90.2 %reduce-scatter.11.cloned.1.call-done = f32[16,1536]{1,0:T(8,128)} async-done(((f32[512,1536]{1,0:T(8,128)}), f32[16,1536]{1,0:T(8,128)}) %reduce-scatter.11.cloned.1.call-update) | async-done | bytes 98320 | tf_op jit(solution)/shard_map/reduce_scatter | solution.py:58
  405.8 1.5 convert_element_type.24
Async XLA Ops:
  7.2 54.3 %copy-start = (bf16[768,1536]{1,0:T(8,128)(2,1)S(1)}, bf16[768,1536]{1,0:T(8,128)(2,1)}, u32[]{:S(2)}) copy-start(bf16[768,1536]{1,0:T(8,128)(2,1)} %param.6) | copy-start | bytes 7077892
  7.2 54.3 %all-gather.5.cloned.1.call-start = ((), (), s32[]{:S(2)}) async-start(), calls=%async_computation.7 | async-start | bytes 1622016 | tf_op jit(solution)/shard_map/all_gather | solution.py:49
  7.9 103.8 %all-gather.3.cloned.1.call-start = ((), (), s32[]{:S(2)}) async-start(), calls=%async_computation.4 | async-start | bytes 1622016 | tf_op jit(solution)/shard_map/all_gather | solution.py:32
  8.7 146.4 %reduce-scatter.9.cloned.1.call-start = ((), (), s32[]{:S(2)}) async-start(), calls=%async_computation.8 | async-start | bytes 1769472 | tf_op jit(solution)/shard_map/reduce_scatter | solution.py:51
  65.5 131.6 %reduce-scatter.5.cloned.1.call-start = ((), (), s32[]{:S(2)}) async-start(), calls=%async_computation.5 | async-start | bytes 1769472 | tf_op jit(solution)/shard_map/reduce_scatter | solution.py:34
  116.4 197.7 %reduce-scatter.7.cloned.1.call-start = ((), (), s32[]{:S(2)}) async-start(), calls=%async_computation.6 | async-start | bytes 3244032 | tf_op jit(solution)/shard_map/reduce_scatter | solution.py:43
  227.4 178.4 %reduce-scatter.11.cloned.1.call-start = ((), (), s32[]{:S(2)}) async-start(), calls=%async_computation.9 | async-start | bytes 3244032 | tf_op jit(solution)/shard_map/reduce_scatter | solution.py:58
  253.2 0.9 copy-start.1
Sparse Core Ops, SparseCore 0:
  10.6 50.8 all-gather.4
  64.0 47.6 all-gather.2
  114.8 40.1 reduce-scatter.8
  158.0 38.9 reduce-scatter.4
  227.5 86.5 reduce-scatter.6
  318.4 87.3 reduce-scatter.10
where the time goes:
time: 415 us; the launch traced here: 414 us
  waiting for transfers between devices  313 us (75%)
  blocking collectives  51.9 us (13%)
  matrix products  25.2 us (6%)
  between operations  14.1 us (3%)
  local copies, waits for them, and re-layouts  5.16 us (1%)
  other arithmetic  4.19 us (1%)
    reduce_scatter x1, waiting for transfers between devices, per_device(): lax.psum_scatter(contract_cols(panel, weight_in), 'row', scatter_dimensio...  90.2 us
    all_gather x1, waiting for transfers between devices, per_device(): cot_all = lax.all_gather(cotangent, 'row', axis=0, tiled=True)  52.8 us
    all_gather x1, waiting for transfers between devices, per_device(): tok_all = lax.all_gather(tokens, 'row', axis=0, tiled=True)  46.2 us
    reduce_scatter x1, waiting for transfers between devices, per_device(): lax.psum_scatter(jnp.dot(panel, weight_out, preferred_element_type=jnp.fl...  42.1 us
    reduce_scatter x1, waiting for transfers between devices, per_device(): lax.psum_scatter(jnp.dot(panel, weight_in, preferred_element_type=jnp.flo...  42 us
    reduce_scatter x1, waiting for transfers between devices, per_device(): lax.psum_scatter(contract_cols(panel, weight_out), 'col', scatter_dimensi...  38.6 us
    all_gather x1, blocking collectives, per_device(): lax.all_gather(gelu_out.astype(jnp.bfloat16), 'col', axis=0, tiled=True)  26.1 us
    all_gather x1, blocking collectives, per_device(): grad_all = lax.all_gather(grad_hidden, 'col', axis=0, tiled=True)  25.8 us
  transfers between devices with their start and end apart: 6, of which 6 were waited for; matrix products, arithmetic and copies ran while one was open for 7% of the time, Pallas kernels for 0%

commit v1 on v0

v1 whole, which is shorter than its diff:
```python
import jax
import jax.numpy as jnp
from jax import lax
from jax.experimental import pallas as pl
from jax.experimental.pallas import tpu as pltpu
from jax.sharding import PartitionSpec as P

MESH = pl.DeviceIdType.MESH
F32, BF16 = jnp.float32, jnp.bfloat16
gelu_scale = 0.7978845608028654
gelu_cubic = 0.044715

NZ = 8
NX = NY = 4
ROWS = 16
TOK = 512
SHARD = TOK // NZ
HALF = SHARD // 2
FEAT = 1536
FH = FEAT // 2
HID = 768
NC = 3
W = HID // NC
N_SEM = 176


def activate(hidden):
    tangent = jnp.tanh(gelu_scale * (hidden + gelu_cubic * hidden * hidden * hidden))
    gelu_out = 0.5 * hidden * (1.0 + tangent)
    derivative = 0.5 * (1.0 + tangent) + 0.5 * hidden * (1.0 - tangent * tangent) * gelu_scale * (
        1.0 + 3.0 * gelu_cubic * hidden * hidden
    )
    return (gelu_out, derivative)


def mm(left, right):
    return lax.dot_general(left, right, (((1,), (0,)), ((), ())), preferred_element_type=F32)


def mm_nt(left, right):
    return lax.dot_general(left, right, (((1,), (1,)), ((), ())), preferred_element_type=F32)


def mm_tn(left, right):
    return lax.dot_general(left, right, (((0,), (0,)), ((), ())), preferred_element_type=F32)


def kernel(
    tok_hbm, wi_hbm, wo_hbm, cot_hbm,
    out_ref, gt_ref, gwi_hbm, gwo_hbm,
    wi, wo, tok, cot, hid, gac, zsnd, zrcv, act, grd, slope,
    psnd, prcv, own, lsnd, lrcv, ssnd, srcv, gwi, gwo,
    ssem, rsem, lsem,
):
    row, z = lax.axis_index("row"), lax.axis_index("col")
    c, x, y = lax.rem(row, 2), lax.rem(row // 2, NX), row // (2 * NX)

    def at(dc, dy, dx, dz):
        yy, xx = lax.rem(y + dy, NY), lax.rem(x + dx, NX)
        cc = 1 - c if dc else c
        return ((yy * NX + xx) * 2 + cc, lax.rem(z + dz, NZ))

    def along(axis, d):
        return at(0, d, 0, 0) if axis == "y" else at(0, 0, d, 0)

    sibling, z_up, z_down = at(1, 0, 0, 0), at(0, 0, 0, 1), at(0, 0, 0, NZ - 1)

    used = [0]
    sends = []

    def send(src, dst, dev):
        i = used[0]
        used[0] += 1
        copy = pltpu.make_async_remote_copy(
            src_ref=src, dst_ref=dst, send_sem=ssem.at[i], recv_sem=rsem.at[i],
            device_id=dev, device_id_type=MESH,
        )
        copy.start()
        sends.append(copy)
        return copy

    local = []

    def fetch(src, dst):
        copy = pltpu.make_async_copy(src, dst, lsem.at[len(local)])
        copy.start()
        local.append(copy)
        return copy

    got_tok = [fetch(tok_hbm.at[:, pl.ds(h * FH, FH)], tok.at[h, 0, 0, 0]) for h in (0, 1)]
    got_cot = [fetch(cot_hbm.at[:, pl.ds(h * FH, FH)], cot.at[h, 0, 0, 0]) for h in (0, 1)]
    got_wi = fetch(wi_hbm, wi)
    got_wo = fetch(wo_hbm, wo)

    barrier = pltpu.get_barrier_semaphore()
    partners = [sibling, z_up, z_down] + [along(a, d) for a in ("x", "y") for d in (1, 2, 3)]
    for dev in partners:
        pl.semaphore_signal(barrier, inc=1, device_id=dev, device_id_type=MESH)
    pl.semaphore_wait(barrier, len(partners))

    first, second = ("x", "y"), ("y", "x")

    def slots(ref, h, dc, da, db):
        sl = [slice(None) if d is None else d for d in (da, db)]
        dy, dx = (sl[1], sl[0]) if first[h] == "x" else (sl[0], sl[1])
        return ref.at[h, dc, dy, dx]

    def gather_first(ref, got):
        a, b = {}, {}
        for h in (0, 1):
            got[h].wait()
            for d in (1, 3, 2):
                a[h, d] = send(slots(ref, h, 0, 0, 0), slots(ref, h, 0, 4 - d, 0), along(first[h], d))
            for d in (1, 3, 2):
                b[h, d] = send(slots(ref, h, 0, 0, 0), slots(ref, h, 0, 0, 4 - d), along(second[h], d))
        return a, b

    def gather_second(ref, a):
        g = {}
        for h in (0, 1):
            for d in (1, 3, 2):
                a[h, d].wait_recv()
            for d in (1, 3, 2):
                dev = along(second[h], d)
                g[h, d] = send(slots3(ref, h, 0), slots3(ref, h, 4 - d), dev)
        return g

    def slots3(ref, h, db):
        if first[h] == "x":
            return ref.at[h, 0, db, pl.ds(1, 3)]
        return ref.at[h, 0, pl.ds(1, 3), db]

    def gather_near(ref):
        return {(h, 0): send(slots(ref, h, 0, None, 0), slots(ref, h, 1, None, 0), sibling) for h in (0, 1)}

    def gather_far(ref, b, g):
        s = {}
        for d in (1, 3, 2):
            for h in (0, 1):
                b[h, d].wait_recv()
                g[h, d].wait_recv()
                e = 4 - d
                s[h, e] = send(slots(ref, h, 0, None, e), slots(ref, h, 1, None, e), sibling)
        return s

    def rows(ref, h):
        return ref[h].reshape(TOK, FH)

    def reduce_step(n, part, j, t, got):
        for way, dev in ((0, z_up), (1, z_down)):
            share = lax.rem(z + (5 - t if way == 0 else 3 + t), NZ)
            near = pl.ds(way * HALF, HALF)
            buf = zsnd.at[n, j, way, t - 1]
            if t == 1:
                buf[near] = part[j, share, near].astype(BF16)
                src, dst = buf.at[near], zrcv.at[n, j, way, t - 1, near]
            else:
                got[way, t - 1].wait_recv()
                if t == 2:
                    far = pl.ds((1 - way) * HALF, HALF)
                    buf[near] = (part[j, share, near] + zrcv[n, j, way, 0, near].astype(F32)).astype(BF16)
                    buf[far] = part[j, share, far].astype(BF16)
                else:
                    buf[...] = (part[j, share] + zrcv[n, j, way, t - 2].astype(F32)).astype(BF16)
                src, dst = buf, zrcv.at[n, j, way, t - 1]
            got[way, t] = send(src, dst, dev)

    def reduce_end(n, part, j, got):
        got[0, 4].wait_recv()
        got[1, 4].wait_recv()
        return part[j, z] + zrcv[n, j, 0, 3].astype(F32) + zrcv[n, j, 1, 3].astype(F32)

    def spread_step(ref, j, t, got):
        for way, dev in ((0, z_up), (1, z_down)):
            share = lax.rem(z + (NZ + 1 - t if way == 0 else t - 1), NZ)
            if t > 1:
                got[way, t - 1].wait_recv()
            block = ref.at[j, share]
            if t == 4:
                block = block.at[pl.ds(way * HALF, HALF)]
            got[way, t] = send(block, block, dev)

    def spread_end(got):
        got[0, 4].wait_recv()
        got[1, 4].wait_recv()

    def scatter_pair(n, h, value):
        own[n, h] = value[: TOK // 2].reshape(NY, NX, ROWS, FH)
        psnd[n, h] = value[TOK // 2 :].reshape(NY, NX, ROWS, FH)
        return send(psnd.at[n, h], prcv.at[n, h], sibling)

    def scatter_first(n, h, got):
        got.wait_recv()
        res = {}
        for d in (2, 1, 3):
            if first[h] == "x":
                val = own[n, h, d] + prcv[n, h, d]
            else:
                val = own[n, h, :, d] + prcv[n, h, :, d]
            lsnd[n, h, d - 1] = val.astype(BF16)
            res[d] = send(lsnd.at[n, h, d - 1], lrcv.at[n, h, d - 1], along(second[h], d))
        if first[h] == "x":
            own[n, h, 0] = own[n, h, 0] + prcv[n, h, 0]
        else:
            own[n, h, :, 0] = own[n, h, :, 0] + prcv[n, h, :, 0]
        return res

    def scatter_second(n, h, got):
        for d in (1, 3, 2):
            got[d].wait_recv()
        res = {}
        base = own[n, h, 0] if first[h] == "x" else own[n, h, :, 0]
        total = base + lrcv[n, h, 0].astype(F32) + lrcv[n, h, 1].astype(F32) + lrcv[n, h, 2].astype(F32)
        ssnd[n, h] = total
        for d in (2, 1, 3):
            res[d] = send(ssnd.at[n, h, d], srcv.at[n, h, d - 1], along(first[h], d))
        return res

    def scatter_end(n, h, got, ref):
        for d in (1, 3, 2):
            got[d].wait_recv()
        total = ssnd[n, h, 0] + srcv[n, h, 0] + srcv[n, h, 1] + srcv[n, h, 2]
        ref[:, pl.ds(h * FH, FH)] = total.astype(BF16)

    chunks = range(NC)

    a, b = gather_first(tok, got_tok)
    ca, cb = gather_first(cot, got_cot)
    g = gather_second(tok, a)
    near = gather_near(tok)
    far = gather_far(tok, b, g)
    cg = gather_second(cot, ca)
    cnear = gather_near(cot)
    got_wi.wait()
    for s in (near, far):
        for copy in s.values():
            copy.wait_recv()

    hg = [{} for _ in chunks]
    gg = [{} for _ in chunks]
    for j in chunks:
        cols = pl.ds(j * W, W)
        value = mm(rows(tok, 0), wi[pl.ds(0, FH), cols]) + mm(rows(tok, 1), wi[pl.ds(FH, FH), cols])
        hid[j] = value.reshape(NZ, SHARD, W)
        reduce_step(0, hid, j, 1, hg[j])
    cfar = gather_far(cot, cb, cg)
    for j in chunks:
        reduce_step(0, hid, j, 2, hg[j])
    got_wo.wait()
    for s in (cnear, cfar):
        for copy in s.values():
            copy.wait_recv()
    for j in chunks:
        cols = pl.ds(j * W, W)
        value = mm_nt(rows(cot, 0), wo[cols, pl.ds(0, FH)]) + mm_nt(rows(cot, 1), wo[cols, pl.ds(FH, FH)])
        gac[j] = value.reshape(NZ, SHARD, W)
        reduce_step(1, gac, j, 1, gg[j])
    for t in (3, 4):
        for j in chunks:
            reduce_step(0, hid, j, t, hg[j])
        for j in chunks:
            reduce_step(1, gac, j, t - 1, gg[j])
    ag = [{} for _ in chunks]
    bg = [{} for _ in chunks]
    for j in chunks:
        gelu_out, derivative = activate(reduce_end(0, hid, j, hg[j]))
        act[j, z] = gelu_out.astype(BF16)
        slope[j] = derivative
        spread_step(act, j, 1, ag[j])
    for j in chunks:
        reduce_step(1, gac, j, 4, gg[j])
    for j in chunks:
        spread_step(act, j, 2, ag[j])
    for j in chunks:
        grd[j, z] = (reduce_end(1, gac, j, gg[j]) * slope[j]).astype(BF16)
        spread_step(grd, j, 1, bg[j])
    for t in (3, 4):
        for j in chunks:
            spread_step(act, j, t, ag[j])
        for j in chunks:
            spread_step(grd, j, t - 1, bg[j])
    for j in chunks:
        spread_end(ag[j])

    op = []
    for h in (0, 1):
        value = jnp.zeros((TOK, FH), F32)
        for j in chunks:
            value = value + mm(act[j].reshape(TOK, W), wo[pl.ds(j * W, W), pl.ds(h * FH, FH)])
        op.append(scatter_pair(0, h, value))
    for j in chunks:
        spread_step(grd, j, 4, bg[j])
    for j in chunks:
        spread_end(bg[j])
    gp = []
    for h in (0, 1):
        value = jnp.zeros((TOK, FH), F32)
        for j in chunks:
            value = value + mm_nt(grd[j].reshape(TOK, W), wi[pl.ds(h * FH, FH), pl.ds(j * W, W)])
        gp.append(scatter_pair(1, h, value))
        if h == 0:
            o1 = [scatter_first(0, k, op[k]) for k in (0, 1)]
    for j in chunks:
        for h in (0, 1):
            gwo[pl.ds(j * W, W), pl.ds(h * FH, FH)] = mm_tn(act[j].reshape(TOK, W), rows(cot, h)).astype(BF16)
    put_gwo = fetch(gwo, gwo_hbm)
    g1 = [scatter_first(1, h, gp[h]) for h in (0, 1)]
    o2 = [scatter_second(0, h, o1[h]) for h in (0, 1)]
    for h in (0, 1):
        for j in chunks:
            gwi[pl.ds(h * FH, FH), pl.ds(j * W, W)] = mm_tn(rows(tok, h), grd[j].reshape(TOK, W)).astype(BF16)
    put_gwi = fetch(gwi, gwi_hbm)
    g2 = [scatter_second(1, h, g1[h]) for h in (0, 1)]
    for h in (0, 1):
        scatter_end(0, h, o2[h], out_ref)
    for h in (0, 1):
        scatter_end(1, h, g2[h], gt_ref)
    put_gwo.wait()
    put_gwi.wait()
    for copy in sends:
        copy.wait_send()
    assert used[0] <= N_SEM, used[0]


def per_device(tokens, weight_in, weight_out, cotangent):
    any_spec = pl.BlockSpec(memory_space=pl.ANY)
    vmem = pl.BlockSpec(memory_space=pltpu.VMEM)
    shape = jax.ShapeDtypeStruct
    return pl.pallas_call(
        kernel,
        out_shape=(
            shape((ROWS, FEAT), BF16), shape((ROWS, FEAT), BF16), shape((FEAT, HID), BF16), shape((HID, FEAT), BF16),
        ),
        in_specs=[any_spec] * 4,
        out_specs=(vmem, vmem, any_spec, any_spec),
        scratch_shapes=[
            pltpu.VMEM((FEAT, HID), BF16),
            pltpu.VMEM((HID, FEAT), BF16),
            pltpu.VMEM((2, 2, NY, NX, ROWS, FH), BF16),
            pltpu.VMEM((2, 2, NY, NX, ROWS, FH), BF16),
            pltpu.VMEM((NC, NZ, SHARD, W), F32),
            pltpu.VMEM((NC, NZ, SHARD, W), F32),
            pltpu.VMEM((2, NC, 2, 4, SHARD, W), BF16),
            pltpu.VMEM((2, NC, 2, 4, SHARD, W), BF16),
            pltpu.VMEM((NC, NZ, SHARD, W), BF16),
            pltpu.VMEM((NC, NZ, SHARD, W), BF16),
            pltpu.VMEM((NC, SHARD, W), F32),
            pltpu.VMEM((2, 2, NY, NX, ROWS, FH), F32),
            pltpu.VMEM((2, 2, NY, NX, ROWS, FH), F32),
            pltpu.VMEM((2, 2, NY, NX, ROWS, FH), F32),
            pltpu.VMEM((2, 2, 3, 4, ROWS, FH), BF16),
            pltpu.VMEM((2, 2, 3, 4, ROWS, FH), BF16),
            pltpu.VMEM((2, 2, 4, ROWS, FH), F32),
            pltpu.VMEM((2, 2, 3, ROWS, FH), F32),
            pltpu.VMEM((FEAT, HID), BF16),
            pltpu.VMEM((HID, FEAT), BF16),
            pltpu.SemaphoreType.DMA((N_SEM,)),
            pltpu.SemaphoreType.DMA((N_SEM,)),
            pltpu.SemaphoreType.DMA((8,)),
        ],
        compiler_params=pltpu.CompilerParams(
            collective_id=0, has_side_effects=True, vmem_limit_bytes=52 * 2**20
        ),
        cost_estimate=pl.CostEstimate(flops=7 * 10**9, bytes_accessed=10**7, transcendentals=5 * 10**4),
    )(tokens, weight_in, weight_out, cotangent)


def solution(mesh):
    in_specs = (P("row", "col"), P("col", "row"), P("row", "col"), P("row", "col"))
    out_specs = (P("row", "col"), P("row", "col"), P("col", "row"), P("row", "col"))
    return jax.shard_map(
        per_device, mesh=mesh, in_specs=in_specs, out_specs=out_specs, check_vma=False
    )
```

time: 415 us -> 89 us (0.21)
  waiting for transfers between devices: 313 us -> 0 us
  Pallas kernels: 0 us -> 79.1 us
  blocking collectives: 51.9 us -> 0 us
  matrix products: 25.2 us -> 0 us
  between operations: 14.1 us -> 0.65 us
  other arithmetic: 4.19 us -> 0 us
    reduce_scatter x4 -> x0, waiting for transfers between devices: 213 us -> none  [the longest x1 90.2 us: per_device(): lax.psum_scatter(contract_cols(panel, weight_in), 'row', scatter_dimensio...]
    all_gather x2 -> x0, waiting for transfers between devices: 99 us -> none  [the longest x1 52.8 us: per_device(): cot_all = lax.all_gather(cotangent, 'row', axis=0, tiled=True)]
    pallas_call x0 -> x1, Pallas kernels: none -> 79.1 us  [per_device(): pl.pallas_call(kernel, out_shape=(shape((ROWS, FEAT), BF16), shape((ROWS,...]
    all_gather x2 -> x0, blocking collectives: 51.9 us -> none  [the longest x1 26.1 us: per_device(): lax.all_gather(gelu_out.astype(jnp.bfloat16), 'col', axis=0, tiled=True)]
    dot_general x6 -> x0, matrix products: 25.2 us -> none  [the longest x2 8.78 us: contract_cols(): lax.dot_general(left, right, (((1,), (1,)), ((), ())), preferred_element_...]
    convert_element_type x3 -> x0, other arithmetic: 4.19 us -> none  [the longest x1 1.52 us: per_device(): output = lax.psum_scatter(jnp.dot(panel, weight_out, preferred_element_ty...]
  transfers between devices with their start and end apart: 6 -> 0, of which waited for: 6 -> 0; matrix products, arithmetic and copies ran while one was open for 7% -> 0% of each run, Pallas kernels for 0% -> 0%
where the time goes in v1:
time: 89 us; the launch traced here: 87.3 us
  Pallas kernels  79.1 us (89%)
  local copies, waits for them, and re-layouts  7.61 us (9%)
    pallas_call x1, Pallas kernels, per_device(): pl.pallas_call(kernel, out_shape=(shape((ROWS, FEAT), BF16), shape((ROWS,...  79.1 us
    unnamed x10, local copies, waits for them, and re-layouts  7.61 us

profile of v1, /device:TPU:2, one launch (start us, length us, event | category | flops | bytes accessed | tf_op | source)
XLA Modules:
  0.0 87.3 jit_solution(6504506734873568933)
XLA Ops:
  0.6 0.0 copy-start
  0.6 0.8 copy-done
  1.4 0.0 copy-start.1
  1.4 0.8 copy-done.1
  2.2 79.1 %shard_map.75 = (bf16[16,1536]{1,0:T(8,128)(2,1)S(1)}, bf16[16,1536]{1,0:T(8,128)(2,1)S(1)}, bf16[1536,768]{1,0:T(8,128)(2,1)}, bf16[768,1536]{1,0:T(8,128)(2,1)}) custom-call(bf16[16,1536]{1,0:T(8,128)(2,1)S(1)} %copy-done, bf16[1536,768]{1,0:T(8,128)(2,1)} %wi_hbm.1, bf16[768,1536]{1,0:T(8,128)(2,1)} %wo_hbm.1, bf16[16,1536]{1,0:T(8,128)(2,1)S(1)} %copy-done.1), custom_call_target="tpu_custom_call" | custom-call | flops 7000000000 | bytes 10000000 | tf_op jit(solution)/shard_map/pallas_call | solution.py:329
  81.3 0.6 copy.12
  81.9 0.6 copy.13
  82.6 0.0 copy-start.2
  82.6 3.4 %copy.14 = bf16[1536,768]{1,0:T(8,128)(2,1)} copy(bf16[1536,768]{1,0:T(8,128)(2,1)} %get-tuple-element.10) | data formatting | bytes 4718592
  85.9 0.0 copy-done.2
  85.9 1.4 %copy.15 = bf16[768,1536]{1,0:T(8,128)(2,1)} copy(bf16[768,1536]{1,0:T(8,128)(2,1)S(1)} %copy-done.2) | data formatting | bytes 4718592
Async XLA Ops:
  0.6 0.8 copy-start
  1.4 0.8 copy-start.1
  82.6 3.4 %copy-start.2 = (bf16[768,1536]{1,0:T(8,128)(2,1)S(1)}, bf16[768,1536]{1,0:T(8,128)(2,1)}, u32[]{:S(2)}) copy-start(bf16[768,1536]{1,0:T(8,128)(2,1)} %get-tuple-element.11) | copy-start | bytes 7077892

commit v2 on v0

v2 whole, which is shorter than its diff:
```python
import jax
import jax.numpy as jnp
from jax import lax
from jax.experimental import pallas as pl
from jax.experimental.pallas import tpu as pltpu
from jax.sharding import PartitionSpec as P

MESH = pl.DeviceIdType.MESH
F32, BF16 = jnp.float32, jnp.bfloat16
gelu_scale = 0.7978845608028654
gelu_cubic = 0.044715

NZ = 8
NX = NY = 4
ROWS = 16
MINE = NY * NX * ROWS
SHARD = MINE // NZ
HALF = SHARD // 2
LINE = NX * ROWS
FEAT = 1536
FH = FEAT // 2
HID = 768


def activate(hidden):
    tangent = jnp.tanh(gelu_scale * (hidden + gelu_cubic * hidden * hidden * hidden))
    gelu_out = 0.5 * hidden * (1.0 + tangent)
    derivative = 0.5 * (1.0 + tangent) + 0.5 * hidden * (1.0 - tangent * tangent) * gelu_scale * (
        1.0 + 3.0 * gelu_cubic * hidden * hidden
    )
    return (gelu_out, derivative)


def mm(left, right):
    return lax.dot_general(left, right, (((1,), (0,)), ((), ())), preferred_element_type=F32)


def mm_nt(left, right):
    return lax.dot_general(left, right, (((1,), (1,)), ((), ())), preferred_element_type=F32)


def mm_tn(left, right):
    return lax.dot_general(left, right, (((0,), (0,)), ((), ())), preferred_element_type=F32)


def kernel(
    tok_hbm, wi_hbm, wo_hbm, cot_hbm,
    out_ref, gt_ref, gwi, gwo,
    wi, wo, wi2, wo2, tok, cot, part, zsnd, zrcv, act, grd, slope, own, lsnd, lrcv, ssnd, srcv,
    ssem, rsem, lsem,
):
    row, z = lax.axis_index("row"), lax.axis_index("col")
    c, x, y = lax.rem(row, 2), lax.rem(row // 2, NX), row // (2 * NX)

    def at(cc, dy, dx, dz):
        return ((lax.rem(y + dy, NY) * NX + lax.rem(x + dx, NX)) * 2 + cc, lax.rem(z + dz, NZ))

    def along(axis, d):
        return at(c, d, 0, 0) if axis == "y" else at(c, 0, d, 0)

    sibling, z_up, z_down = at(1 - c, 0, 0, 0), at(c, 0, 0, 1), at(c, 0, 0, NZ - 1)

    names = {}

    def sem(pool, name):
        known = names.setdefault(id(pool), {})
        return pool.at[known.setdefault(name, len(known))]

    def copy_to(src, dst, s, r, dev):
        return pltpu.make_async_remote_copy(
            src_ref=src, dst_ref=dst, send_sem=sem(ssem, s), recv_sem=sem(rsem, r),
            device_id=dev, device_id_type=MESH,
        )

    sent = {}

    def send(src, dst, s, r, dev):
        copy_to(src, dst, s, r, dev).start()
        size = 1
        for n in src.shape:
            size *= n
        sent[s] = sent.get(s, 0) + size * src.dtype.itemsize

    def arrived(like, r):
        copy_to(like, like, "none", r, sibling).wait_recv()

    def all_sent(s):
        n = sent[s] // (HID * 2)
        assert n * HID * 2 == sent[s] and n <= FEAT, (s, n)
        copy_to(wi.at[pl.ds(0, n)], wi.at[pl.ds(0, n)], s, "none", sibling).wait_send()

    def fetch(src, dst, name):
        copy = pltpu.make_async_copy(src, dst, sem(lsem, name))
        copy.start()
        return copy

    got_tok = fetch(tok_hbm, tok.at[pl.ds(0, ROWS)], "tok")
    got_cot = fetch(cot_hbm, cot.at[pl.ds(0, ROWS)], "cot")
    got_wi = fetch(wi_hbm, wi, "wi")
    got_wo = fetch(wo_hbm, wo, "wo")

    barrier = pltpu.get_barrier_semaphore()
    partners = [sibling, z_up, z_down] + [along(a, d) for a in ("x", "y") for d in (1, 2, 3)]
    for dev in partners:
        pl.semaphore_signal(barrier, inc=1, device_id=dev, device_id_type=MESH)
    pl.semaphore_wait(barrier, len(partners))

    first, second = ("x", "y"), ("y", "x")

    def block(ref, h, da, db):
        dy, dx = (db, da) if first[h] == "x" else (da, db)
        return ref.at[pl.ds((dy * NX + dx) * ROWS, ROWS), pl.ds(h * FH, FH)]

    def gather_first(ref, name):
        for h in (0, 1):
            for d in (1, 3, 2):
                send(block(ref, h, 0, 0), block(ref, h, 4 - d, 0), "gather", (name, "a", h), along(first[h], d))
        for h in (0, 1):
            for d in (1, 3, 2):
                send(block(ref, h, 0, 0), block(ref, h, 0, 4 - d), "gather", (name, "b"), along(second[h], d))

    def gather_second(ref, name):
        for h in (0, 1):
            arrived(ref.at[pl.ds(ROWS, 3 * ROWS), pl.ds(h * FH, FH)], (name, "a", h))
            for d in (1, 3, 2):
                if first[h] == "x":
                    cols = pl.ds(h * FH, FH)
                    send(
                        ref.at[pl.ds(ROWS, 3 * ROWS), cols], ref.at[pl.ds((4 - d) * LINE + ROWS, 3 * ROWS), cols],
                        "gather", (name, "b"), along(second[h], d),
                    )
                else:
                    for e in (1, 2, 3):
                        send(block(ref, h, e, 0), block(ref, h, e, 4 - d), "gather", (name, "b"), along(second[h], d))

    def gather_end(ref, name):
        arrived(ref.at[pl.ds(LINE, 3 * LINE)], (name, "b"))

    def share_rows(dz):
        return pl.ds(pl.multiple_of(lax.rem(z + dz, NZ) * SHARD, SHARD), SHARD)

    def half_rows(dz, way):
        return pl.ds(pl.multiple_of(lax.rem(z + dz, NZ) * SHARD + way * HALF, HALF), HALF)

    def reduce_step(n, k, t):
        if t > 1:
            arrived(zrcv.at[n, k, t - 2, 0] if t == 2 else zrcv.at[n, k, t - 2], ("r", n, k, t - 1))
        for way, dev in ((0, z_up), (1, z_down)):
            dz = 5 - t if way == 0 else 3 + t
            near, far = pl.ds(way * HALF, HALF), pl.ds((1 - way) * HALF, HALF)
            buf, dst = zsnd.at[n, k, t - 1, way], zrcv.at[n, k, t - 1, way]
            if t == 1:
                buf[near] = part[n, k, half_rows(dz, way)].astype(BF16)
                buf, dst = buf.at[near], dst.at[near]
            elif t == 2:
                buf[near] = (part[n, k, half_rows(dz, way)] + zrcv[n, k, 0, way, near].astype(F32)).astype(BF16)
                buf[far] = part[n, k, half_rows(dz, 1 - way)].astype(BF16)
            else:
                buf[...] = (part[n, k, share_rows(dz)] + zrcv[n, k, t - 2, way].astype(F32)).astype(BF16)
            send(buf, dst, ("z", n), ("r", n, k, t), dev)

    def reduce_end(n, k):
        arrived(zrcv.at[n, k, 3], ("r", n, k, 4))
        return part[n, k, share_rows(0)] + zrcv[n, k, 3, 0].astype(F32) + zrcv[n, k, 3, 1].astype(F32)

    def spread_step(n, ref, k, t):
        if t > 1:
            arrived(zrcv.at[n, k, 3], ("s", n, k, t - 1))
        for way, dev in ((0, z_up), (1, z_down)):
            dz = NZ + 1 - t if way == 0 else t - 1
            piece = ref.at[2 * k, half_rows(dz, way) if t == 4 else share_rows(dz)]
            send(piece, piece, ("z", n), ("s", n, k, t), dev)

    def spread_end(n, k):
        arrived(zrcv.at[n, k, 3, 0], ("s", n, k, 4))

    def scatter_first(n, h, value):
        for d in (2, 1, 3, 0):
            if first[h] == "x":
                val = value[d * LINE : (d + 1) * LINE]
            else:
                val = jnp.concatenate([value[e * LINE + d * ROWS : e * LINE + (d + 1) * ROWS] for e in range(NY)], axis=0)
            if d == 0:
                own[n, h] = val
            else:
                lsnd[n, h, d - 1] = val.astype(BF16)
                send(lsnd.at[n, h, d - 1], lrcv.at[n, h, d - 1], ("l", n), ("l", n, h), along(second[h], d))

    def scatter_second(n, h):
        arrived(lrcv.at[n, h], ("l", n, h))
        ssnd[n, h] = own[n, h] + lrcv[n, h, 0].astype(F32) + lrcv[n, h, 1].astype(F32) + lrcv[n, h, 2].astype(F32)
        for d in (2, 1, 3):
            rows = pl.ds(d * ROWS, ROWS)
            send(ssnd.at[n, h, rows], srcv.at[n, h, d - 1], ("l", n), ("m", n, h), along(first[h], d))

    def scatter_end(n, h, ref):
        arrived(srcv.at[n, h], ("m", n, h))
        total = ssnd[n, h, pl.ds(0, ROWS)] + srcv[n, h, 0] + srcv[n, h, 1] + srcv[n, h, 2]
        ref[:, pl.ds(h * FH, FH)] = total.astype(BF16)

    mine, theirs = pl.ds(0, MINE), pl.ds(MINE, MINE)
    halves = (0, 1)

    got_tok.wait()
    gather_first(tok, "tok")
    got_wi.wait()
    send(wi, wi2, "wi", "wi", sibling)
    got_cot.wait()
    gather_first(cot, "cot")
    got_wo.wait()
    send(wo, wo2, "wo", "wo", sibling)
    gather_second(tok, "tok")
    gather_end(tok, "tok")
    gather_second(cot, "cot")

    part[0, 0] = mm(tok[mine], wi[...])
    reduce_step(0, 0, 1)
    arrived(wi2, "wi")
    part[0, 1] = mm(tok[mine], wi2[...])
    reduce_step(0, 1, 1)
    reduce_step(0, 0, 2)
    reduce_step(0, 1, 2)
    gather_end(cot, "cot")
    part[1, 0] = mm_nt(cot[mine], wo[...])
    reduce_step(1, 0, 1)
    arrived(wo2, "wo")
    part[1, 1] = mm_nt(cot[mine], wo2[...])
    reduce_step(1, 1, 1)
    send(tok.at[mine], tok.at[theirs], "near", "tok2", sibling)
    send(cot.at[mine], cot.at[theirs], "near", "cot2", sibling)
    for t in (3, 4):
        for k in halves:
            reduce_step(0, k, t)
        for k in halves:
            reduce_step(1, k, t - 1)
    for k in halves:
        gelu_out, derivative = activate(reduce_end(0, k))
        act[2 * k, share_rows(0)] = gelu_out.astype(BF16)
        slope[k] = derivative
        spread_step(0, act, k, 1)
    for k in halves:
        reduce_step(1, k, 4)
    for k in halves:
        spread_step(0, act, k, 2)
    for k in halves:
        grd[2 * k, share_rows(0)] = (reduce_end(1, k) * slope[k]).astype(BF16)
        spread_step(1, grd, k, 1)
    for t in (3, 4):
        for k in halves:
            spread_step(0, act, k, t)
        for k in halves:
            spread_step(1, grd, k, t - 1)
    for k in halves:
        spread_end(0, k)
    send(act.at[2], act.at[1], "near", "act2", sibling)
    for h in halves:
        cols = pl.ds(h * FH, FH)
        scatter_first(0, h, mm(act[0], wo[:, cols]) + mm(act[2], wo2[:, cols]))
        spread_step(1, grd, h, 4)
    arrived(tok.at[theirs], "tok2")
    arrived(cot.at[theirs], "cot2")
    arrived(act.at[1], "act2")
    gwo[...] = mm_tn(act[pl.ds(0, 2)].reshape(2 * MINE, HID), cot[...]).astype(BF16)
    for k in halves:
        spread_end(1, k)
    send(grd.at[2], grd.at[1], "near", "grd2", sibling)
    for h in halves:
        cols = pl.ds(h * FH, FH)
        scatter_first(1, h, mm_nt(grd[0], wi[cols, :]) + mm_nt(grd[2], wi2[cols, :]))
    for h in halves:
        scatter_second(0, h)
    arrived(grd.at[1], "grd2")
    gwi[...] = mm_tn(tok[...], grd[pl.ds(0, 2)].reshape(2 * MINE, HID)).astype(BF16)
    for h in halves:
        scatter_second(1, h)
    for h in halves:
        scatter_end(0, h, out_ref)
    for h in halves:
        scatter_end(1, h, gt_ref)
    for s in sent:
        all_sent(s)
    for pool, known in ((ssem, 12), (rsem, 64), (lsem, 4)):
        assert len(names[id(pool)]) <= known


def hand_over(*refs):
    srcs, dsts, sems = refs[:4], refs[4:8], refs[8]
    copies = []
    for s, d in zip(srcs, dsts):
        parts = s.shape[0] // 192 or 1
        for p in range(parts):
            rows = pl.ds(p * (s.shape[0] // parts), s.shape[0] // parts)
            copies.append(pltpu.make_async_copy(s.at[rows], d.at[rows], sems.at[len(copies)]))
    for copy in copies:
        copy.start()
    for copy in copies:
        copy.wait()


def per_device(tokens, weight_in, weight_out, cotangent):
    hbm = pl.BlockSpec(memory_space=pltpu.HBM)
    vmem = pl.BlockSpec(memory_space=pltpu.VMEM)
    shape = jax.ShapeDtypeStruct
    shapes = (
        shape((ROWS, FEAT), BF16), shape((ROWS, FEAT), BF16), shape((FEAT, HID), BF16), shape((HID, FEAT), BF16),
    )
    tokens, cotangent = [pltpu.with_memory_space_constraint(a, pltpu.HBM) for a in (tokens, cotangent)]
    results = pl.pallas_call(
        kernel,
        out_shape=shapes,
        in_specs=[hbm] * 4,
        out_specs=(vmem,) * 4,
        scratch_shapes=[
            pltpu.VMEM((FEAT, HID), BF16),
            pltpu.VMEM((HID, FEAT), BF16),
            pltpu.VMEM((FEAT, HID), BF16),
            pltpu.VMEM((HID, FEAT), BF16),
            pltpu.VMEM((2 * MINE, FEAT), BF16),
            pltpu.VMEM((2 * MINE, FEAT), BF16),
            pltpu.VMEM((2, 2, MINE, HID), F32),
            pltpu.VMEM((2, 2, 4, 2, SHARD, HID), BF16),
            pltpu.VMEM((2, 2, 4, 2, SHARD, HID), BF16),
            pltpu.VMEM((3, MINE, HID), BF16),
            pltpu.VMEM((3, MINE, HID), BF16),
            pltpu.VMEM((2, SHARD, HID), F32),
            pltpu.VMEM((2, 2, LINE, FH), F32),
            pltpu.VMEM((2, 2, 3, LINE, FH), BF16),
            pltpu.VMEM((2, 2, 3, LINE, FH), BF16),
            pltpu.VMEM((2, 2, LINE, FH), F32),
            pltpu.VMEM((2, 2, 3, ROWS, FH), F32),
            pltpu.SemaphoreType.DMA((12,)),
            pltpu.SemaphoreType.DMA((64,)),
            pltpu.SemaphoreType.DMA((4,)),
        ],
        compiler_params=pltpu.CompilerParams(
            collective_id=0, has_side_effects=True, vmem_limit_bytes=48 * 2**20
        ),
        cost_estimate=pl.CostEstimate(flops=7 * 10**9, bytes_accessed=10**7, transcendentals=5 * 10**4),
    )(tokens, weight_in, weight_out, cotangent)
    return pl.pallas_call(
        hand_over,
        out_shape=shapes,
        in_specs=[vmem] * 4,
        out_specs=(hbm,) * 4,
        scratch_shapes=[pltpu.SemaphoreType.DMA((14,))],
        compiler_params=pltpu.CompilerParams(vmem_limit_bytes=2**21),
        cost_estimate=pl.CostEstimate(flops=0, bytes_accessed=10**7, transcendentals=0),
    )(*results)


def solution(mesh):
    in_specs = (P("row", "col"), P("col", "row"), P("row", "col"), P("row", "col"))
    out_specs = (P("row", "col"), P("row", "col"), P("col", "row"), P("row", "col"))
    return jax.shard_map(
        per_device, mesh=mesh, in_specs=in_specs, out_specs=out_specs, check_vma=False
    )
```

time: 415 us -> 73.7 us (0.18)
  waiting for transfers between devices: 313 us -> 0 us
  Pallas kernels: 0 us -> 73 us
  blocking collectives: 51.9 us -> 0 us
  matrix products: 25.2 us -> 0 us
  between operations: 14.1 us -> 0.64 us
  local copies, waits for them, and re-layouts: 5.16 us -> 0 us
  other arithmetic: 4.19 us -> 0 us
    reduce_scatter x4 -> x0, waiting for transfers between devices: 213 us -> none  [the longest x1 90.2 us: per_device(): lax.psum_scatter(contract_cols(panel, weight_in), 'row', scatter_dimensio...]
    all_gather x2 -> x0, waiting for transfers between devices: 99 us -> none  [the longest x1 52.8 us: per_device(): cot_all = lax.all_gather(cotangent, 'row', axis=0, tiled=True)]
    pallas_call x0 -> x2, Pallas kernels: none -> 73 us  [the longest x1 70.7 us: per_device(): pl.pallas_call(kernel, out_shape=shapes, in_specs=[hbm] * 4, out_specs=(v...]
    all_gather x2 -> x0, blocking collectives: 51.9 us -> none  [the longest x1 26.1 us: per_device(): lax.all_gather(gelu_out.astype(jnp.bfloat16), 'col', axis=0, tiled=True)]
    dot_general x6 -> x0, matrix products: 25.2 us -> none  [the longest x2 8.78 us: contract_cols(): lax.dot_general(left, right, (((1,), (1,)), ((), ())), preferred_element_...]
    unnamed x5 -> x0, local copies, waits for them, and re-layouts: 5.16 us -> none
    convert_element_type x3 -> x0, other arithmetic: 4.19 us -> none  [the longest x1 1.52 us: per_device(): output = lax.psum_scatter(jnp.dot(panel, weight_out, preferred_element_ty...]
  transfers between devices with their start and end apart: 6 -> 0, of which waited for: 6 -> 0; matrix products, arithmetic and copies ran while one was open for 7% -> 0% of each run, Pallas kernels for 0% -> 0%
where the time goes in v2:
time: 73.7 us; the launch traced here: 73.6 us
  Pallas kernels  73 us (99%)
    pallas_call x1, Pallas kernels, per_device(): pl.pallas_call(kernel, out_shape=shapes, in_specs=[hbm] * 4, out_specs=(v...  70.7 us
    pallas_call x1, Pallas kernels, per_device(): pl.pallas_call(hand_over, out_shape=shapes, in_specs=[vmem] * 4, out_spec...  2.33 us

profile of v2, /device:TPU:2, one launch (start us, length us, event | category | flops | bytes accessed | tf_op | source)
XLA Modules:
  0.0 73.6 jit_solution(15057600812820728620)
XLA Ops:
  0.6 70.7 %shard_map.75 = (bf16[16,1536]{1,0:T(8,128)(2,1)S(1)}, bf16[16,1536]{1,0:T(8,128)(2,1)S(1)}, bf16[1536,768]{1,0:T(8,128)(2,1)S(1)}, bf16[768,1536]{1,0:T(8,128)(2,1)S(1)}) custom-call(bf16[16,1536]{1,0:T(8,128)(2,1)} %tok_hbm.1, bf16[1536,768]{1,0:T(8,128)(2,1)} %wi_hbm.1, bf16[768,1536]{1,0:T(8,128)(2,1)} %wo_hbm.1, bf16[16,1536]{1,0:T(8,128)(2,1)} %cot_hbm.1), custom_call_target="tpu_custom_call" | custom-call | flops 7000000000 | bytes 10000000 | tf_op jit(solution)/shard_map/pallas_call | solution.py:308
  71.3 2.3 %shard_map.76 = (bf16[16,1536]{1,0:T(8,128)(2,1)}, bf16[16,1536]{1,0:T(8,128)(2,1)}, bf16[1536,768]{1,0:T(8,128)(2,1)}, bf16[768,1536]{1,0:T(8,128)(2,1)}) custom-call(bf16[16,1536]{1,0:T(8,128)(2,1)S(1)} %get-tuple-element.8.refs_0_, bf16[16,1536]{1,0:T(8,128)(2,1)S(1)} %get-tuple-element.9.refs_1_, bf16[1536,768]{1,0:T(8,128)(2,1)S(1)} %get-tuple-element.10.refs_2_, ...), custom_call_target="tpu_custom_call" | custom-call | bytes 10000000 | tf_op jit(solution)/shard_map/pallas_call | solution.py:340

commit v3 on v0

v3 whole, which is shorter than its diff:
```python
import jax
import jax.numpy as jnp
from jax import lax
from jax.experimental import pallas as pl
from jax.experimental.pallas import tpu as pltpu
from jax.sharding import PartitionSpec as P

MESH = pl.DeviceIdType.MESH
F32, BF16 = jnp.float32, jnp.bfloat16
gelu_scale = 0.7978845608028654
gelu_cubic = 0.044715

NZ = 8
NX = NY = 4
ROWS = 16
MINE = NY * NX * ROWS
CHUNK = MINE // 2
PAIR = 2 * ROWS
FEAT = 1536
FH = FEAT // 2
HID = 768
N_SEND, N_RECV = 12, 72


def activate(hidden):
    tangent = jnp.tanh(gelu_scale * (hidden + gelu_cubic * hidden * hidden * hidden))
    gelu_out = 0.5 * hidden * (1.0 + tangent)
    derivative = 0.5 * (1.0 + tangent) + 0.5 * hidden * (1.0 - tangent * tangent) * gelu_scale * (
        1.0 + 3.0 * gelu_cubic * hidden * hidden
    )
    return (gelu_out, derivative)


def mm(left, right):
    return lax.dot_general(left, right, (((1,), (0,)), ((), ())), preferred_element_type=F32)


def mm_tn(left, right):
    return lax.dot_general(left, right, (((0,), (0,)), ((), ())), preferred_element_type=F32)


def kernel(
    tok_hbm, wi_hbm, wo_hbm, cot_hbm,
    out_ref, gt_ref, gwi, gwo,
    wi, wo, wit, wot, tok, cot, part, zsnd, zrcv, act, grd, act2, grd2, slope, tmp, own, lsnd, lrcv, ssnd, srcv,
    ssem, rsem, lsem,
):
    row, z = lax.axis_index("row"), lax.axis_index("col")
    c, x, y = lax.rem(row, 2), lax.rem(row // 2, NX), row // (2 * NX)
    parity = lax.rem(x + y, 2)
    stages = halves = (0, 1)
    chunk = [lax.rem(r + parity, 2) for r in stages]

    def at(cc, dy, dx, dz):
        return ((lax.rem(y + dy, NY) * NX + lax.rem(x + dx, NX)) * 2 + cc, lax.rem(z + dz, NZ))

    def along(axis, d):
        return at(c, d, 0, 0) if axis == "y" else at(c, 0, d, 0)

    sibling, z_up, z_down = at(1 - c, 0, 0, 0), at(c, 0, 0, 1), at(c, 0, 0, NZ - 1)

    names = {}

    def sem(pool, name):
        known = names.setdefault(id(pool), {})
        return pool.at[known.setdefault(name, len(known))]

    def copy_to(src, dst, s, r, dev):
        return pltpu.make_async_remote_copy(
            src_ref=src, dst_ref=dst, send_sem=sem(ssem, s), recv_sem=sem(rsem, r),
            device_id=dev, device_id_type=MESH,
        )

    sent = {}

    def send(src, dst, s, r, dev, counts=True):
        copy_to(src, dst, s, r, dev).start()
        size = src.dtype.itemsize if counts else 0
        for n in src.shape:
            size *= n
        sent[s] = sent.get(s, 0) + size

    def arrived(like, r):
        copy_to(like, like, "none", r, sibling).wait_recv()

    def all_sent(s):
        n = sent[s] // (HID * 2)
        assert n * HID * 2 == sent[s] and n <= FEAT, (s, n)
        like = wi.at[pl.ds(0, n), pl.ds(0, HID)]
        copy_to(like, like, s, "none", sibling).wait_send()

    def fetch(src, dst, name):
        copy = pltpu.make_async_copy(src, dst, sem(lsem, name))
        copy.start()
        return copy

    def rows16(i):
        return pl.ds(i * ROWS if isinstance(i, int) else pl.multiple_of(i * ROWS, ROWS), ROWS)

    mine, theirs = pl.ds(0, HID), pl.ds(HID, HID)

    got_tok = fetch(tok_hbm, tok.at[0, rows16(0)], "tok")
    got_cot = fetch(cot_hbm, cot.at[0, rows16(0)], "cot")
    got_wi = fetch(wi_hbm, wi.at[:, mine], "wi")
    got_wo = fetch(wo_hbm, wo.at[mine], "wo")

    barrier = pltpu.get_barrier_semaphore()
    partners = [sibling, z_up, z_down] + [along(a, d) for a in ("x", "y") for d in (1, 2, 3)]
    for dev in partners:
        pl.semaphore_signal(barrier, inc=1, device_id=dev, device_id_type=MESH)
    pl.semaphore_wait(barrier, len(partners))

    first, second = ("x", "y"), ("y", "x")
    cols = [pl.ds(h * FH, FH) for h in halves]

    def gather_first(ref, name):
        for h in halves:
            for d in (1, 3, 2):
                dst = rows16((4 - d) // 2 if first[h] == "x" else (4 - d) * 2)
                send(ref.at[0, rows16(0), cols[h]], ref.at[d % 2, dst, cols[h]], "gather", (name, "a", h), along(first[h], d))

    def gather_first_end(ref, name):
        for h in halves:
            arrived(ref.at[0, pl.ds(0, 3 * ROWS), cols[h]], (name, "a", h))

    def gather_second(ref, name, r):
        q = chunk[r]
        for d in (1, 3, 2):
            there = lax.rem(q + d, 2)
            send(
                ref.at[q, pl.ds(0, PAIR), cols[0]], ref.at[there, pl.ds((4 - d) * PAIR, PAIR), cols[0]],
                "gather", (name, "b", r), along(second[0], d),
            )
            for e in (0, 2):
                send(
                    ref.at[q, rows16((q + e) * 2), cols[1]], ref.at[there, rows16((q + e) * 2 + (4 - d) // 2), cols[1]],
                    "gather", (name, "b", r), along(second[1], d),
                )

    def gather_end(ref, name, r):
        arrived(ref.at[0, pl.ds(0, 3 * PAIR)], (name, "b", r))

    def share(dz):
        return rows16(lax.rem(z + dz, NZ))

    def reduce_step(n, r, t):
        if t > 1:
            arrived(zrcv.at[n, r, 0, 0] if t == 2 else zrcv.at[n, r, t - 2], ("r", n, r, t - 1))
        for way, dev in ((0, z_up), (1, z_down)):
            dz = 5 - t if way == 0 else 3 + t
            near, far = (mine, theirs) if way == 0 else (theirs, mine)
            buf, dst = zsnd.at[n, r, t - 1, way], zrcv.at[n, r, t - 1, way]
            if t == 1:
                buf[:, near] = part[n, r, share(dz), near].astype(BF16)
                buf, dst = buf.at[:, near], dst.at[:, near]
            elif t == 2:
                buf[:, near] = (part[n, r, share(dz), near] + zrcv[n, r, 0, way, :, near].astype(F32)).astype(BF16)
                buf[:, far] = part[n, r, share(dz), far].astype(BF16)
            else:
                buf[...] = (part[n, r, share(dz)] + zrcv[n, r, t - 2, way].astype(F32)).astype(BF16)
            send(buf, dst, ("z", n), ("r", n, r, t), dev)

    def reduce_end(n, r):
        arrived(zrcv.at[n, r, 3], ("r", n, r, 4))
        return part[n, r, share(0)] + zrcv[n, r, 3, 0].astype(F32) + zrcv[n, r, 3, 1].astype(F32)

    def spread_step(n, r, t):
        ref = grd if n else act
        if t > 1:
            arrived(zrcv.at[n, r, 3], ("s", n, r, t - 1))
        for way, dev in ((0, z_up), (1, z_down)):
            piece = ref.at[chunk[r], share(NZ + 1 - t if way == 0 else t - 1)]
            if t == 4:
                piece = piece.at[:, theirs if way else mine]
            send(piece, piece, ("z", n), ("s", n, r, t), dev)

    def spread_end(n, r):
        arrived(zrcv.at[n, r, 3, 0], ("s", n, r, 4))
        ref, dst = (grd, grd2) if n else (act, act2)
        send(ref.at[chunk[r], :, theirs], dst.at[chunk[r]], "near", ("near", n), sibling)

    def scatter_first(n, r, h, value):
        if h == 1:
            tmp[...] = value
        for d in (2, 1, 3, 0):
            if h == 0:
                val = value[d * PAIR : (d + 1) * PAIR]
            else:
                f = lax.rem(chunk[r] + d, 2)
                val = jnp.concatenate([tmp[rows16((f + e) * 2 + d // 2)] for e in (0, 2)], axis=0)
            if d == 0:
                own[n, r, h] = val
            else:
                lsnd[n, r, h, d - 1] = val.astype(BF16)
                send(lsnd.at[n, r, h, d - 1], lrcv.at[n, r, h, d - 1], ("l", n), ("l", n, r, h), along(second[h], d))

    def scatter_second(n, r):
        q = chunk[r]
        for h in halves:
            arrived(lrcv.at[n, r, h], ("l", n, r, h))
            got = [lrcv[n, r, h, d].astype(F32) for d in (0, 1, 2)]
            ssnd[n, r, h] = own[n, r, h] + got[0] + got[1] + got[2]
            send(ssnd.at[n, r, h, rows16(1)], srcv.at[n, h, q + 1], ("l", n), ("m", n, h), along(first[h], q + 2))

            @pl.when(q == 1)
            def _():
                send(ssnd.at[n, r, h, rows16(0)], srcv.at[n, h, 0], ("l", n), ("m", n, h), along(first[h], 1), r == 0)

    def scatter_end(n, ref):
        for h in halves:
            arrived(srcv.at[n, h], ("m", n, h))
            total = ssnd[n, parity, h, rows16(0)] + srcv[n, h, 0] + srcv[n, h, 1] + srcv[n, h, 2]
            ref[:, cols[h]] = total.astype(BF16)

    def multiply(n, r):
        if n == 0:
            part[0, r] = mm(tok[chunk[r]], wi[...])
        else:
            part[1, r] = mm(cot[chunk[r]], wot[...])
        reduce_step(n, r, 1)

    def middle(n, r):
        total = reduce_end(n, r)
        if n == 0:
            gelu_out, derivative = activate(total)
            act[chunk[r], share(0)] = gelu_out.astype(BF16)
            slope[r] = derivative
        else:
            grd[chunk[r], share(0)] = (total * slope[r]).astype(BF16)
        spread_step(n, r, 1)

    def finish(n, r):
        spread_end(n, r)
        for h in halves:
            if n == 0:
                scatter_first(n, r, h, mm(act[chunk[r]], wo[:, cols[h]]))
            else:
                scatter_first(n, r, h, mm(grd[chunk[r]], wit[:, cols[h]]))

    def both(ref, first_chunk):
        got = ref[pl.ds(first_chunk, 2)]
        return got.reshape(-1, got.shape[-1])

    def weight_grad(n):
        if n == 0:
            arrived(cot.at[pl.ds(2, 2)], "cot2")
            arrived(act2, ("near", 0))
            total = mm_tn(act[:, :, mine].reshape(MINE, HID), both(cot, 0)) + mm_tn(both(act2, 0), both(cot, 2))
            gwo[...] = total.astype(BF16)
        else:
            arrived(tok.at[pl.ds(2, 2)], "tok2")
            arrived(grd2, ("near", 1))
            total = mm_tn(both(tok, 0), grd[:, :, mine].reshape(MINE, HID)) + mm_tn(both(tok, 2), both(grd2, 0))
            gwi[...] = total.astype(BF16)

    got_tok.wait()
    gather_first(tok, "tok")
    got_wi.wait()
    send(wi.at[:, mine], wi.at[:, theirs], "wi", "wi", sibling)
    got_cot.wait()
    gather_first(cot, "cot")
    got_wo.wait()
    for i in range(3):
        wot[:, pl.ds(i * 256, 256)] = wo[pl.ds(i * 256, 256)].T
    send(wot.at[:, mine], wot.at[:, theirs], "wot", "wot", sibling)
    gather_first_end(tok, "tok")
    gather_second(tok, "tok", 0)
    gather_second(tok, "tok", 1)
    for i in range(3):
        wit[pl.ds(i * 256, 256)] = wi[:, pl.ds(i * 256, 256)].T
    send(wo.at[mine], wo.at[theirs], "wo", "wo", sibling)
    send(wit.at[mine], wit.at[theirs], "wit", "wit", sibling)
    gather_first_end(cot, "cot")
    gather_end(tok, "tok", 0)
    gather_second(cot, "cot", 0)
    arrived(wi.at[:, theirs], "wi")
    multiply(0, 0)
    gather_end(tok, "tok", 1)
    gather_second(cot, "cot", 1)
    multiply(0, 1)
    reduce_step(0, 0, 2)
    gather_end(cot, "cot", 0)
    arrived(wot.at[:, theirs], "wot")
    multiply(1, 0)
    reduce_step(0, 1, 2)
    gather_end(cot, "cot", 1)
    multiply(1, 1)
    send(tok.at[pl.ds(0, 2)], tok.at[pl.ds(2, 2)], "near", "tok2", sibling)
    send(cot.at[pl.ds(0, 2)], cot.at[pl.ds(2, 2)], "near", "cot2", sibling)
    reduce_step(0, 0, 3)
    reduce_step(1, 0, 2)
    reduce_step(0, 1, 3)
    reduce_step(1, 1, 2)
    reduce_step(0, 0, 4)
    reduce_step(1, 0, 3)
    reduce_step(0, 1, 4)
    reduce_step(1, 1, 3)
    middle(0, 0)
    reduce_step(1, 0, 4)
    middle(0, 1)
    reduce_step(1, 1, 4)
    spread_step(0, 0, 2)
    middle(1, 0)
    spread_step(0, 1, 2)
    middle(1, 1)
    spread_step(0, 0, 3)
    spread_step(1, 0, 2)
    spread_step(0, 1, 3)
    spread_step(1, 1, 2)
    spread_step(0, 0, 4)
    spread_step(1, 0, 3)
    spread_step(0, 1, 4)
    spread_step(1, 1, 3)
    arrived(wo.at[theirs], "wo")
    finish(0, 0)
    spread_step(1, 0, 4)
    finish(0, 1)
    spread_step(1, 1, 4)
    arrived(wit.at[theirs], "wit")
    finish(1, 0)
    scatter_second(0, 0)
    finish(1, 1)
    scatter_second(0, 1)
    weight_grad(0)
    scatter_second(1, 0)
    weight_grad(1)
    scatter_second(1, 1)
    scatter_end(0, out_ref)
    scatter_end(1, gt_ref)
    for s in sent:
        all_sent(s)
    for pool, known in ((ssem, N_SEND), (rsem, N_RECV), (lsem, 4)):
        assert len(names[id(pool)]) <= known, len(names[id(pool)])


def hand_over(*refs):
    srcs, dsts, sems = refs[:4], refs[4:8], refs[8]
    copies = []
    for s, d in zip(srcs, dsts):
        parts = s.shape[0] // 192 or 1
        for p in range(parts):
            rows = pl.ds(p * (s.shape[0] // parts), s.shape[0] // parts)
            copies.append(pltpu.make_async_copy(s.at[rows], d.at[rows], sems.at[len(copies)]))
    for copy in copies:
        copy.start()
    for copy in copies:
        copy.wait()


def per_device(tokens, weight_in, weight_out, cotangent):
    hbm = pl.BlockSpec(memory_space=pltpu.HBM)
    vmem = pl.BlockSpec(memory_space=pltpu.VMEM)
    shape = jax.ShapeDtypeStruct
    shapes = (
        shape((ROWS, FEAT), BF16), shape((ROWS, FEAT), BF16), shape((FEAT, HID), BF16), shape((HID, FEAT), BF16),
    )
    tokens, cotangent = [pltpu.with_memory_space_constraint(a, pltpu.HBM) for a in (tokens, cotangent)]
    results = pl.pallas_call(
        kernel,
        out_shape=shapes,
        in_specs=[hbm] * 4,
        out_specs=(vmem,) * 4,
        scratch_shapes=[
            pltpu.VMEM((FEAT, 2 * HID), BF16),
            pltpu.VMEM((2 * HID, FEAT), BF16),
            pltpu.VMEM((2 * HID, FEAT), BF16),
            pltpu.VMEM((FEAT, 2 * HID), BF16),
            pltpu.VMEM((4, CHUNK, FEAT), BF16),
            pltpu.VMEM((4, CHUNK, FEAT), BF16),
            pltpu.VMEM((2, 2, CHUNK, 2 * HID), F32),
            pltpu.VMEM((2, 2, 4, 2, ROWS, 2 * HID), BF16),
            pltpu.VMEM((2, 2, 4, 2, ROWS, 2 * HID), BF16),
            pltpu.VMEM((2, CHUNK, 2 * HID), BF16),
            pltpu.VMEM((2, CHUNK, 2 * HID), BF16),
            pltpu.VMEM((2, CHUNK, HID), BF16),
            pltpu.VMEM((2, CHUNK, HID), BF16),
            pltpu.VMEM((2, ROWS, 2 * HID), F32),
            pltpu.VMEM((CHUNK, FH), F32),
            pltpu.VMEM((2, 2, 2, PAIR, FH), F32),
            pltpu.VMEM((2, 2, 2, 3, PAIR, FH), BF16),
            pltpu.VMEM((2, 2, 2, 3, PAIR, FH), BF16),
            pltpu.VMEM((2, 2, 2, PAIR, FH), F32),
            pltpu.VMEM((2, 2, 3, ROWS, FH), F32),
            pltpu.SemaphoreType.DMA((N_SEND,)),
            pltpu.SemaphoreType.DMA((N_RECV,)),
            pltpu.SemaphoreType.DMA((4,)),
        ],
        compiler_params=pltpu.CompilerParams(
            collective_id=0, has_side_effects=True, vmem_limit_bytes=48 * 2**20
        ),
        cost_estimate=pl.CostEstimate(flops=7 * 10**9, bytes_accessed=10**7, transcendentals=5 * 10**4),
    )(tokens, weight_in, weight_out, cotangent)
    return pl.pallas_call(
        hand_over,
        out_shape=shapes,
        in_specs=[vmem] * 4,
        out_specs=(hbm,) * 4,
        scratch_shapes=[pltpu.SemaphoreType.DMA((14,))],
        compiler_params=pltpu.CompilerParams(vmem_limit_bytes=2**21),
        cost_estimate=pl.CostEstimate(flops=0, bytes_accessed=10**7, transcendentals=0),
    )(*results)


def solution(mesh):
    in_specs = (P("row", "col"), P("col", "row"), P("row", "col"), P("row", "col"))
    out_specs = (P("row", "col"), P("row", "col"), P("col", "row"), P("row", "col"))
    return jax.shard_map(
        per_device, mesh=mesh, in_specs=in_specs, out_specs=out_specs, check_vma=False
    )
```

time: 415 us -> 69.5 us (0.17)
  waiting for transfers between devices: 313 us -> 0 us
  Pallas kernels: 0 us -> 68.7 us
  blocking collectives: 51.9 us -> 0 us
  matrix products: 25.2 us -> 0 us
  between operations: 14.1 us -> 0.64 us
  local copies, waits for them, and re-layouts: 5.16 us -> 0 us
  other arithmetic: 4.19 us -> 0 us
    reduce_scatter x4 -> x0, waiting for transfers between devices: 213 us -> none  [the longest x1 90.2 us: per_device(): lax.psum_scatter(contract_cols(panel, weight_in), 'row', scatter_dimensio...]
    all_gather x2 -> x0, waiting for transfers between devices: 99 us -> none  [the longest x1 52.8 us: per_device(): cot_all = lax.all_gather(cotangent, 'row', axis=0, tiled=True)]
    pallas_call x0 -> x2, Pallas kernels: none -> 68.7 us  [the longest x1 66.4 us: per_device(): pl.pallas_call(kernel, out_shape=shapes, in_specs=[hbm] * 4, out_specs=(v...]
    all_gather x2 -> x0, blocking collectives: 51.9 us -> none  [the longest x1 26.1 us: per_device(): lax.all_gather(gelu_out.astype(jnp.bfloat16), 'col', axis=0, tiled=True)]
    dot_general x6 -> x0, matrix products: 25.2 us -> none  [the longest x2 8.78 us: contract_cols(): lax.dot_general(left, right, (((1,), (1,)), ((), ())), preferred_element_...]
    unnamed x5 -> x0, local copies, waits for them, and re-layouts: 5.16 us -> none
    convert_element_type x3 -> x0, other arithmetic: 4.19 us -> none  [the longest x1 1.52 us: per_device(): output = lax.psum_scatter(jnp.dot(panel, weight_out, preferred_element_ty...]
  transfers between devices with their start and end apart: 6 -> 0, of which waited for: 6 -> 0; matrix products, arithmetic and copies ran while one was open for 7% -> 0% of each run, Pallas kernels for 0% -> 0%
where the time goes in v3:
time: 69.5 us; the launch traced here: 69.4 us
  Pallas kernels  68.7 us (99%)
    pallas_call x1, Pallas kernels, per_device(): pl.pallas_call(kernel, out_shape=shapes, in_specs=[hbm] * 4, out_specs=(v...  66.4 us
    pallas_call x1, Pallas kernels, per_device(): pl.pallas_call(hand_over, out_shape=shapes, in_specs=[vmem] * 4, out_spec...  2.33 us

profile of v3, /device:TPU:2, one launch (start us, length us, event | category | flops | bytes accessed | tf_op | source)
XLA Modules:
  0.0 69.4 jit_solution(7244983927085627674)
XLA Ops:
  0.6 66.4 %shard_map.75 = (bf16[16,1536]{1,0:T(8,128)(2,1)S(1)}, bf16[16,1536]{1,0:T(8,128)(2,1)S(1)}, bf16[1536,768]{1,0:T(8,128)(2,1)S(1)}, bf16[768,1536]{1,0:T(8,128)(2,1)S(1)}) custom-call(bf16[16,1536]{1,0:T(8,128)(2,1)} %tok_hbm.1, bf16[1536,768]{1,0:T(8,128)(2,1)} %wi_hbm.1, bf16[768,1536]{1,0:T(8,128)(2,1)} %wo_hbm.1, bf16[16,1536]{1,0:T(8,128)(2,1)} %cot_hbm.1), custom_call_target="tpu_custom_call" | custom-call | flops 7000000000 | bytes 10000000 | tf_op jit(solution)/shard_map/pallas_call | solution.py:358
  67.1 2.3 %shard_map.76 = (bf16[16,1536]{1,0:T(8,128)(2,1)}, bf16[16,1536]{1,0:T(8,128)(2,1)}, bf16[1536,768]{1,0:T(8,128)(2,1)}, bf16[768,1536]{1,0:T(8,128)(2,1)}) custom-call(bf16[16,1536]{1,0:T(8,128)(2,1)S(1)} %get-tuple-element.8.refs_0_, bf16[16,1536]{1,0:T(8,128)(2,1)S(1)} %get-tuple-element.9.refs_1_, bf16[1536,768]{1,0:T(8,128)(2,1)S(1)} %get-tuple-element.10.refs_2_, ...), custom_call_target="tpu_custom_call" | custom-call | bytes 10000000 | tf_op jit(solution)/shard_map/pallas_call | solution.py:393

commit v4 on v3

--- a/solution.py
+++ b/solution.py
@@ -19,7 +19,7 @@
 FEAT = 1536
 FH = FEAT // 2
 HID = 768
-N_SEND, N_RECV = 12, 72
+N_SEND, N_RECV = 10, 56
 
 
 def activate(hidden):
@@ -42,7 +42,7 @@
 def kernel(
     tok_hbm, wi_hbm, wo_hbm, cot_hbm,
     out_ref, gt_ref, gwi, gwo,
-    wi, wo, wit, wot, tok, cot, part, zsnd, zrcv, act, grd, act2, grd2, slope, tmp, own, lsnd, lrcv, ssnd, srcv,
+    wi, wo, wit, wot, tok, cot, part, zsnd, zrcv, act, grd, act2, grd2, slope, lsnd, lrcv, ssnd, srcv,
     ssem, rsem, lsem,
 ):
     row, z = lax.axis_index("row"), lax.axis_index("col")
@@ -58,6 +58,7 @@
         return at(c, d, 0, 0) if axis == "y" else at(c, 0, d, 0)
 
     sibling, z_up, z_down = at(1 - c, 0, 0, 0), at(c, 0, 0, 1), at(c, 0, 0, NZ - 1)
+    z_up2, z_down2 = at(c, 0, 0, 2), at(c, 0, 0, NZ - 2)
 
     names = {}
 
@@ -81,13 +82,13 @@
         sent[s] = sent.get(s, 0) + size
 
     def arrived(like, r):
-        copy_to(like, like, "none", r, sibling).wait_recv()
+        copy_to(like, like, "wi", r, sibling).wait_recv()
 
     def all_sent(s):
         n = sent[s] // (HID * 2)
         assert n * HID * 2 == sent[s] and n <= FEAT, (s, n)
         like = wi.at[pl.ds(0, n), pl.ds(0, HID)]
-        copy_to(like, like, s, "none", sibling).wait_send()
+        copy_to(like, like, s, "wi", sibling).wait_send()
 
     def fetch(src, dst, name):
         copy = pltpu.make_async_copy(src, dst, sem(lsem, name))
@@ -105,7 +106,7 @@
     got_wo = fetch(wo_hbm, wo.at[mine], "wo")
 
     barrier = pltpu.get_barrier_semaphore()
-    partners = [sibling, z_up, z_down] + [along(a, d) for a in ("x", "y") for d in (1, 2, 3)]
+    partners = [sibling, z_up, z_down, z_up2, z_down2] + [along(a, d) for a in ("x", "y") for d in (1, 2, 3)]
     for dev in partners:
         pl.semaphore_signal(barrier, inc=1, device_id=dev, device_id_type=MESH)
     pl.semaphore_wait(barrier, len(partners))
@@ -144,18 +145,29 @@
         return rows16(lax.rem(z + dz, NZ))
 
     def reduce_step(n, r, t):
-        if t > 1:
+        if t == 3 and n == 0:
+            arrived(tok.at[0, pl.ds(0, 3 * ROWS)], ("r", n, r, 1))
+        elif t > 1:
             arrived(zrcv.at[n, r, 0, 0] if t == 2 else zrcv.at[n, r, t - 2], ("r", n, r, t - 1))
-        for way, dev in ((0, z_up), (1, z_down)):
+        for way, dev, dev2 in ((0, z_up, z_up2), (1, z_down, z_down2)):
             dz = 5 - t if way == 0 else 3 + t
-            near, far = (mine, theirs) if way == 0 else (theirs, mine)
+            near = mine if way == 0 else theirs
             buf, dst = zsnd.at[n, r, t - 1, way], zrcv.at[n, r, t - 1, way]
             if t == 1:
                 buf[:, near] = part[n, r, share(dz), near].astype(BF16)
                 buf, dst = buf.at[:, near], dst.at[:, near]
-            elif t == 2:
-                buf[:, near] = (part[n, r, share(dz), near] + zrcv[n, r, 0, way, :, near].astype(F32)).astype(BF16)
-                buf[:, far] = part[n, r, share(dz), far].astype(BF16)
+                if n == 0:
+                    send(buf, dst, ("z", n), ("r", n, r, 1), dev2)
+                    buf, dst = zsnd.at[n, r, 1, way], zrcv.at[n, r, 1, way]
+                    buf[...] = part[n, r, share(3 if way == 0 else 5)].astype(BF16)
+            elif t == 2 or (t == 3 and n == 0):
+                there = zrcv[n, r, 1, way].astype(F32) if n == 0 else 0.0
+                total = part[n, r, share(dz)] + there
+                a, b = total[:, : HID], total[:, HID:]
+                extra = zrcv[n, r, 0, way, :, near].astype(F32)
+                a, b = (a + extra, b) if way == 0 else (a, b + extra)
+                buf[:, mine] = a.astype(BF16)
+                buf[:, theirs] = b.astype(BF16)
             else:
                 buf[...] = (part[n, r, share(dz)] + zrcv[n, r, t - 2, way].astype(F32)).astype(BF16)
             send(buf, dst, ("z", n), ("r", n, r, t), dev)
@@ -169,37 +181,50 @@
         if t > 1:
             arrived(zrcv.at[n, r, 3], ("s", n, r, t - 1))
         for way, dev in ((0, z_up), (1, z_down)):
-            piece = ref.at[chunk[r], share(NZ + 1 - t if way == 0 else t - 1)]
+            dz = NZ + 1 - t if way == 0 else t - 1
+            piece = ref.at[chunk[r], share(dz)]
+            near = theirs if way else mine
+            if t == 3 and n == 1:
+                send(piece.at[:, near], piece.at[:, near], ("z", n), ("s", n, r, t), z_down2 if way else z_up2)
             if t == 4:
-                piece = piece.at[:, theirs if way else mine]
+                piece = piece.at[:, near]
             send(piece, piece, ("z", n), ("s", n, r, t), dev)
+        for dz in (0,) if t == 1 else (NZ + 1 - t, t - 1):
+            hand_near(n, r, dz)
 
     def spread_end(n, r):
-        arrived(zrcv.at[n, r, 3, 0], ("s", n, r, 4))
+        if n == 0:
+            arrived(zrcv.at[n, r, 3, 0], ("s", n, r, 4))
+        else:
+            arrived(tok.at[0, pl.ds(0, 3 * ROWS)], ("s", n, r, 3))
+            hand_near(n, r, 3)
+            hand_near(n, r, 5)
+        hand_near(n, r, 4)
+
+    def hand_near(n, r, dz):
         ref, dst = (grd, grd2) if n else (act, act2)
-        send(ref.at[chunk[r], :, theirs], dst.at[chunk[r]], "near", ("near", n), sibling)
-
-    def scatter_first(n, r, h, value):
-        if h == 1:
-            tmp[...] = value
-        for d in (2, 1, 3, 0):
+        send(ref.at[chunk[r], share(dz), theirs], dst.at[chunk[r], share(dz)], "near", ("near", n), sibling)
+
+    def scatter_first(n, r, h):
+        for d in (2, 1, 3):
             if h == 0:
-                val = value[d * PAIR : (d + 1) * PAIR]
+                lsnd[n, r, h, d - 1] = part[n, r, pl.ds(d * PAIR, PAIR), cols[h]].astype(BF16)
             else:
                 f = lax.rem(chunk[r] + d, 2)
-                val = jnp.concatenate([tmp[rows16((f + e) * 2 + d // 2)] for e in (0, 2)], axis=0)
-            if d == 0:
-                own[n, r, h] = val
-            else:
-                lsnd[n, r, h, d - 1] = val.astype(BF16)
-                send(lsnd.at[n, r, h, d - 1], lrcv.at[n, r, h, d - 1], ("l", n), ("l", n, r, h), along(second[h], d))
+                for i, e in enumerate((0, 2)):
+                    lsnd[n, r, h, d - 1, rows16(i)] = part[n, r, rows16((f + e) * 2 + d // 2), cols[h]].astype(BF16)
+            send(lsnd.at[n, r, h, d - 1], lrcv.at[n, r, h, d - 1], ("l", n), ("l", n, r, h), along(second[h], d))
 
     def scatter_second(n, r):
         q = chunk[r]
         for h in halves:
             arrived(lrcv.at[n, r, h], ("l", n, r, h))
             got = [lrcv[n, r, h, d].astype(F32) for d in (0, 1, 2)]
-            ssnd[n, r, h] = own[n, r, h] + got[0] + got[1] + got[2]
+            if h == 0:
+                own = part[n, r, pl.ds(0, PAIR), cols[h]]
+            else:
+                own = jnp.concatenate([part[n, r, rows16((q + e) * 2), cols[h]] for e in (0, 2)], axis=0)
+            ssnd[n, r, h] = own + got[0] + got[1] + got[2]
             send(ssnd.at[n, r, h, rows16(1)], srcv.at[n, h, q + 1], ("l", n), ("m", n, h), along(first[h], q + 2))
 
             @pl.when(q == 1)
@@ -233,9 +258,10 @@
         spread_end(n, r)
         for h in halves:
             if n == 0:
-                scatter_first(n, r, h, mm(act[chunk[r]], wo[:, cols[h]]))
+                part[n, r, :, cols[h]] = mm(act[chunk[r]], wo[:, cols[h]])
             else:
-                scatter_first(n, r, h, mm(grd[chunk[r]], wit[:, cols[h]]))
+                part[n, r, :, cols[h]] = mm(grd[chunk[r]], wit[:, cols[h]])
+            scatter_first(n, r, h)
 
     def both(ref, first_chunk):
         got = ref[pl.ds(first_chunk, 2)]
@@ -278,44 +304,40 @@
     gather_end(tok, "tok", 1)
     gather_second(cot, "cot", 1)
     multiply(0, 1)
-    reduce_step(0, 0, 2)
     gather_end(cot, "cot", 0)
     arrived(wot.at[:, theirs], "wot")
     multiply(1, 0)
-    reduce_step(0, 1, 2)
+    reduce_step(0, 0, 3)
     gather_end(cot, "cot", 1)
     multiply(1, 1)
     send(tok.at[pl.ds(0, 2)], tok.at[pl.ds(2, 2)], "near", "tok2", sibling)
     send(cot.at[pl.ds(0, 2)], cot.at[pl.ds(2, 2)], "near", "cot2", sibling)
-    reduce_step(0, 0, 3)
+    reduce_step(0, 1, 3)
     reduce_step(1, 0, 2)
-    reduce_step(0, 1, 3)
+    reduce_step(0, 0, 4)
     reduce_step(1, 1, 2)
-    reduce_step(0, 0, 4)
+    reduce_step(0, 1, 4)
     reduce_step(1, 0, 3)
-    reduce_step(0, 1, 4)
+    middle(0, 0)
     reduce_step(1, 1, 3)
-    middle(0, 0)
+    middle(0, 1)
     reduce_step(1, 0, 4)
-    middle(0, 1)
+    spread_step(0, 0, 2)
     reduce_step(1, 1, 4)
-    spread_step(0, 0, 2)
+    spread_step(0, 1, 2)
     middle(1, 0)
-    spread_step(0, 1, 2)
+    spread_step(0, 0, 3)
     middle(1, 1)
-    spread_step(0, 0, 3)
+    spread_step(0, 1, 3)
     spread_step(1, 0, 2)
-    spread_step(0, 1, 3)
+    spread_step(0, 0, 4)
     spread_step(1, 1, 2)
-    spread_step(0, 0, 4)
+    spread_step(0, 1, 4)
     spread_step(1, 0, 3)
-    spread_step(0, 1, 4)
-    spread_step(1, 1, 3)
     arrived(wo.at[theirs], "wo")
     finish(0, 0)
-    spread_step(1, 0, 4)
+    spread_step(1, 1, 3)
     finish(0, 1)
-    spread_step(1, 1, 4)
     arrived(wit.at[theirs], "wit")
     finish(1, 0)
     scatter_second(0, 0)
@@ -375,8 +397,6 @@
             pltpu.VMEM((2, CHUNK, HID), BF16),
             pltpu.VMEM((2, CHUNK, HID), BF16),
             pltpu.VMEM((2, ROWS, 2 * HID), F32),
-            pltpu.VMEM((CHUNK, FH), F32),
-            pltpu.VMEM((2, 2, 2, PAIR, FH), F32),
             pltpu.VMEM((2, 2, 2, 3, PAIR, FH), BF16),
             pltpu.VMEM((2, 2, 2, 3, PAIR, FH), BF16),
             pltpu.VMEM((2, 2, 2, PAIR, FH), F32),

time: 69.5 us -> 67.9 us (0.977)
  Pallas kernels: 68.7 us -> 67.2 us
    pallas_call x1, Pallas kernels: 66.4 us -> 64.9 us  [per_device(): pl.pallas_call(kernel, out_shape=shapes, in_specs=[hbm] * 4, out_specs=(v...]
where the time goes in v4:
time: 67.9 us
  Pallas kernels  67.2 us (99%)
    pallas_call x1, Pallas kernels, per_device(): pl.pallas_call(kernel, out_shape=shapes, in_specs=[hbm] * 4, out_specs=(v...  64.9 us
    pallas_call x1, Pallas kernels, per_device(): pl.pallas_call(hand_over, out_shape=shapes, in_specs=[vmem] * 4, out_spec...  2.33 us

profile of v4, /device:TPU:2, one launch (start us, length us, event | category | flops | bytes accessed | tf_op | source)
XLA Modules:
  0.0 67.9 jit_solution(17384332774938642645)
XLA Ops:
  0.6 64.9 %shard_map.75 = (bf16[16,1536]{1,0:T(8,128)(2,1)S(1)}, bf16[16,1536]{1,0:T(8,128)(2,1)S(1)}, bf16[1536,768]{1,0:T(8,128)(2,1)S(1)}, bf16[768,1536]{1,0:T(8,128)(2,1)S(1)}) custom-call(bf16[16,1536]{1,0:T(8,128)(2,1)} %tok_hbm.1, bf16[1536,768]{1,0:T(8,128)(2,1)} %wi_hbm.1, bf16[768,1536]{1,0:T(8,128)(2,1)} %wo_hbm.1, bf16[16,1536]{1,0:T(8,128)(2,1)} %cot_hbm.1), custom_call_target="tpu_custom_call" | custom-call | flops 7000000000 | bytes 10000000 | tf_op jit(solution)/shard_map/pallas_call | solution.py:380
  65.5 2.3 %shard_map.76 = (bf16[16,1536]{1,0:T(8,128)(2,1)}, bf16[16,1536]{1,0:T(8,128)(2,1)}, bf16[1536,768]{1,0:T(8,128)(2,1)}, bf16[768,1536]{1,0:T(8,128)(2,1)}) custom-call(bf16[16,1536]{1,0:T(8,128)(2,1)S(1)} %get-tuple-element.8.refs_0_, bf16[16,1536]{1,0:T(8,128)(2,1)S(1)} %get-tuple-element.9.refs_1_, bf16[1536,768]{1,0:T(8,128)(2,1)S(1)} %get-tuple-element.10.refs_2_, ...), custom_call_target="tpu_custom_call" | custom-call | bytes 10000000 | tf_op jit(solution)/shard_map/pallas_call | solution.py:413

commit v5 on v4

--- a/solution.py
+++ b/solution.py
@@ -116,7 +116,7 @@
 
     def gather_first(ref, name):
         for h in halves:
-            for d in (1, 3, 2):
+            for d in (2, 1, 3):
                 dst = rows16((4 - d) // 2 if first[h] == "x" else (4 - d) * 2)
                 send(ref.at[0, rows16(0), cols[h]], ref.at[d % 2, dst, cols[h]], "gather", (name, "a", h), along(first[h], d))
 
@@ -126,7 +126,7 @@
 
     def gather_second(ref, name, r):
         q = chunk[r]
-        for d in (1, 3, 2):
+        for d in (2, 1, 3):
             there = lax.rem(q + d, 2)
             send(
                 ref.at[q, pl.ds(0, PAIR), cols[0]], ref.at[there, pl.ds((4 - d) * PAIR, PAIR), cols[0]],
@@ -340,11 +340,11 @@
     finish(0, 1)
     arrived(wit.at[theirs], "wit")
     finish(1, 0)
+    finish(1, 1)
     scatter_second(0, 0)
-    finish(1, 1)
-    scatter_second(0, 1)
     weight_grad(0)
     scatter_second(1, 0)
+    scatter_second(0, 1)
     weight_grad(1)
     scatter_second(1, 1)
     scatter_end(0, out_ref)

time: 67.9 us -> 67 us (0.987)
  Pallas kernels: 67.2 us -> 66.3 us
    pallas_call x1, Pallas kernels: 64.9 us -> 64 us  [per_device(): pl.pallas_call(kernel, out_shape=shapes, in_specs=[hbm] * 4, out_specs=(v...]
where the time goes in v5:
time: 67 us
  Pallas kernels  66.3 us (99%)
    pallas_call x1, Pallas kernels, per_device(): pl.pallas_call(kernel, out_shape=shapes, in_specs=[hbm] * 4, out_specs=(v...  64 us
    pallas_call x1, Pallas kernels, per_device(): pl.pallas_call(hand_over, out_shape=shapes, in_specs=[vmem] * 4, out_spec...  2.33 us

profile of v5, /device:TPU:2, one launch (start us, length us, event | category | flops | bytes accessed | tf_op | source)
XLA Modules:
  0.0 67.0 jit_solution(358521619005644521)
XLA Ops:
  0.6 64.0 %shard_map.75 = (bf16[16,1536]{1,0:T(8,128)(2,1)S(1)}, bf16[16,1536]{1,0:T(8,128)(2,1)S(1)}, bf16[1536,768]{1,0:T(8,128)(2,1)S(1)}, bf16[768,1536]{1,0:T(8,128)(2,1)S(1)}) custom-call(bf16[16,1536]{1,0:T(8,128)(2,1)} %tok_hbm.1, bf16[1536,768]{1,0:T(8,128)(2,1)} %wi_hbm.1, bf16[768,1536]{1,0:T(8,128)(2,1)} %wo_hbm.1, bf16[16,1536]{1,0:T(8,128)(2,1)} %cot_hbm.1), custom_call_target="tpu_custom_call" | custom-call | flops 7000000000 | bytes 10000000 | tf_op jit(solution)/shard_map/pallas_call | solution.py:380
  64.6 2.3 %shard_map.76 = (bf16[16,1536]{1,0:T(8,128)(2,1)}, bf16[16,1536]{1,0:T(8,128)(2,1)}, bf16[1536,768]{1,0:T(8,128)(2,1)}, bf16[768,1536]{1,0:T(8,128)(2,1)}) custom-call(bf16[16,1536]{1,0:T(8,128)(2,1)S(1)} %get-tuple-element.8.refs_0_, bf16[16,1536]{1,0:T(8,128)(2,1)S(1)} %get-tuple-element.9.refs_1_, bf16[1536,768]{1,0:T(8,128)(2,1)S(1)} %get-tuple-element.10.refs_2_, ...), custom_call_target="tpu_custom_call" | custom-call | bytes 10000000 | tf_op jit(solution)/shard_map/pallas_call | solution.py:413
